TPU v7x, 32 devices: a whole 2x2x4 slice. The times are simulated.
32 devices in a mesh: dp: 8 (over y, x, core), tensor: 4 (over z).
Axes of the slice: x: 2, y: 2, z: 4, core: 2. Of those that a mesh axis runs over, the one named last changes fastest.
Arguments:
- hidden: bfloat16 [768, 2560], P('dp', 'tensor'), may hold values from -6 to 6
- grad_out: bfloat16 [768, 4096], P(('dp', 'tensor')), may hold values from -6 to 6
- base_down: bfloat16 [2560, 4096], P('tensor'), may hold values from -0.125 to 0.125
- adapter_in: bfloat16 [2560, 128], P('tensor'), may hold values from -0.125 to 0.125
- adapter_out: bfloat16 [128, 4096], replicated, may hold values from -0.09375 to 0.09375
- mix_ids: int32 [768], P('dp'), may hold values from 0 to 15
- comp_index: int32 [16, 2], replicated, may hold values from 0 to 7
- comp_coef: float32 [16, 2], replicated, may hold values from -1.5 to 1.5
Outputs:
- grad_hidden: bfloat16 [768, 2560], P('dp', 'tensor')
- grad_adapter_in: float32 [2560, 128], P('tensor')
- grad_adapter_out: float32 [128, 4096], replicated
All inputs are finite; a program needn't handle non-finite values.
Results may differ from a plain program's by a relative error of at most 0.0034.
Values may be sent and summed in bfloat16 or wider, within the bound.
A program may use at most 64 MiB of HBM per device.

v0:
```python
import jax
import jax.numpy as jnp
from jax import lax
from jax.sharding import PartitionSpec as P

ADAPTERS = 8
RANK = 16
COMBOS = 16
PICKS = 2


def table_rows(mix_ids, comp_index, comp_coef):
    adapter_ids = jnp.arange(ADAPTERS, dtype=jnp.int32)
    coef_table = jnp.zeros((COMBOS, ADAPTERS), jnp.float32)
    for pick in range(PICKS):
        hits = (comp_index[:, pick : pick + 1] == adapter_ids[None, :]).astype(jnp.float32)
        coef_table = coef_table + comp_coef[:, pick : pick + 1] * hits
    one_hot = (mix_ids[:, None] == jnp.arange(COMBOS, dtype=jnp.int32)[None, :]).astype(jnp.float32)
    per_token = jnp.dot(one_hot, coef_table, precision=lax.Precision.HIGHEST)
    return jnp.repeat(per_token, RANK, axis=1)


def contract_last(left, right):
    return lax.dot_general(
        left, right, (((1,), (1,)), ((), ())), preferred_element_type=jnp.float32
    )


def contract_first(left, right):
    return lax.dot_general(
        left, right, (((0,), (0,)), ((), ())), preferred_element_type=jnp.float32
    )


def whole_form(gathered, low_grads, hidden, base_down, adapter_in, acts):
    grad_hidden = (
        contract_last(gathered, base_down) + contract_last(low_grads, adapter_in)
    ).astype(jnp.bfloat16)
    part_a = contract_first(hidden, low_grads)
    return (grad_hidden, part_a, contract_first(acts, gathered))


def shards(hidden, grad_out, base_down, adapter_in, adapter_out, mix_ids, comp_index, comp_coef):
    group_rows = hidden.shape[0]
    grad_scale = float(group_rows * lax.axis_size("dp")) ** (-0.5)
    mix = table_rows(mix_ids, comp_index, comp_coef)
    acts = None
    low_acts = lax.psum(jnp.dot(hidden, adapter_in, preferred_element_type=jnp.float32), "tensor")
    acts = (low_acts * mix).astype(jnp.bfloat16)
    gathered = lax.all_gather(grad_out, "tensor", axis=0, tiled=True)
    low_grads = (contract_last(gathered, adapter_out) * mix).astype(jnp.bfloat16)
    grad_hidden, part_a, folded_b = whole_form(
        gathered, low_grads, hidden, base_down, adapter_in, acts
    )
    total_a, total_b = lax.psum((part_a, folded_b), "dp")
    return (grad_hidden, total_a * grad_scale, total_b * grad_scale)


def solution(mesh):
    in_specs = (
        P("dp", "tensor"),
        P(("dp", "tensor"), None),
        P("tensor", None),
        P("tensor", None),
        P(),
        P("dp"),
        P(),
        P(),
    )
    out_specs = (P("dp", "tensor"), P("tensor", None), P())
    return jax.shard_map(shards, mesh=mesh, in_specs=in_specs, out_specs=out_specs, check_vma=False)
```

profile of v0, /device:TPU:0, one launch (start us, length us, event | category | flops | bytes accessed | tf_op | source)
XLA Modules:
  0.0 127.3 jit_solution(12154782402542047408)
XLA Ops:
  7.2 0.0 copy-start
  7.2 0.0 copy-start.2
  7.2 0.0 all-reduce.3.cloned.1.call-start
  7.2 0.8 slice_bitcast_fusion.3
  8.0 0.8 slice_bitcast_fusion.2
  8.8 0.9 fusion.2
  9.7 0.1 copy.13
  9.8 1.2 fusion.15
  11.1 21.6 %psum.22 = f32[96,128]{0,1:T(8,128)S(1)} all-reduce(f32[96,128]{0,1:T(8,128)S(1)} %fusion.15), channel_id=1, replica_groups=mesh['dp'=8,'tensor'=4] {'tensor'}, use_global_device_ids=true, to_apply=%region_1.0 | all-reduce | flops 12288 | bytes 98304 | tf_op jit(solution)/shard_map/psum | solution.py:48
  32.7 16.7 %all_gather.3 = bf16[96,4096]{1,0:T(8,128)(2,1)S(1)} all-gather(bf16[24,4096]{1,0:T(8,128)(2,1)} %param.9), channel_id=1, replica_groups=mesh['dp'=8,'tensor'=4] {'tensor'}, dimensions={0}, use_global_device_ids=true | all-gather | bytes 983040 | tf_op jit(solution)/shard_map/all_gather | solution.py:50
  49.4 0.0 copy-done
  49.4 0.5 fusion.1
  49.9 0.0 copy-done.2
  49.9 0.9 convolution_bitcast_fusion
  50.8 1.7 %fusion.3 = f32[128,4096]{1,0:T(8,128)} fusion(bf16[96,4096]{1,0:T(8,128)(2,1)S(1)} %all_gather.3, f32[96,128]{0,1:T(8,128)S(1)} %psum.22, f32[96,128]{0,1:T(8,128)S(1)} %bitcast.23), kind=kOutput, calls=%fused_computation.10 | convolution fusion | flops 100687872 | bytes 2981888 | tf_op jit(solution)/shard_map/dot_general | solution.py:30
  52.6 0.0 all-reduce.3.cloned.1.call-update
  52.6 0.0 copy-start.1
  52.6 4.2 %fusion.14 = f32[96,640]{1,0:T(8,128)S(1)} fusion(bf16[96,4096]{1,0:T(8,128)(2,1)S(1)} %all_gather.3, bf16[640,4096]{1,0:T(8,128)(2,1)} %param.10), kind=kOutput, calls=%fused_computation.27 | convolution fusion | flops 503316480 | bytes 6275072 | tf_op jit(solution)/shard_map/dot_general | solution.py:24
  56.8 0.0 copy-done.1
  56.8 0.9 fusion
  57.7 57.7 %all-reduce.3.cloned.1.call-done = (f32[640,128]{0,1:T(8,128)}, f32[128,4096]{1,0:T(8,128)}) async-done(((f32[640,128]{0,1:T(8,128)}, f32[128,4096]{1,0:T(8,128)}), (f32[640,128]{0,1:T(8,128)}, f32[128,4096]{1,0:T(8,128)})) %all-reduce.3.cloned.1.call-update) | async-done | bytes 2424848 | tf_op jit(solution)/shard_map/psum | solution.py:55
  115.4 1.0 broadcast_multiply_fusion.1
  116.4 0.9 copy.14
  117.3 3.1 %broadcast_multiply_fusion = f32[128,4096]{1,0:T(8,128)} fusion(f32[128,4096]{1,0:T(8,128)} %get-tuple-element.10), kind=kLoop, calls=%fused_computation.5 | loop fusion | flops 524288 | bytes 4194304 | tf_op jit(solution)/shard_map/mul | solution.py:56
  (1 shorter events, 0.0 us)
Async XLA Ops:
  7.2 42.2 %copy-start = (bf16[128,4096]{1,0:T(8,128)(2,1)S(1)}, bf16[128,4096]{1,0:T(8,128)(2,1)}, u32[]{:S(2)}) copy-start(bf16[128,4096]{1,0:T(8,128)(2,1)} %param.12) | copy-start | bytes 3145732
  7.2 42.7 %copy-start.2 = (bf16[96,640]{1,0:T(8,128)(2,1)S(1)}, bf16[96,640]{1,0:T(8,128)(2,1)}, u32[]{:S(2)}) copy-start(bf16[96,640]{1,0:T(8,128)(2,1)} %param.8) | copy-start | bytes 368644
  7.2 108.2 %all-reduce.3.cloned.1.call-start = ((), (), s32[]{:S(2)}) async-start(), calls=%async_computation | async-start | bytes 4849664 | tf_op jit(solution)/shard_map/psum | solution.py:55
  52.6 4.2 %copy-start.1 = (bf16[640,128]{1,0:T(8,128)(2,1)S(1)}, bf16[640,128]{1,0:T(8,128)(2,1)}, u32[]{:S(2)}) copy-start(bf16[640,128]{1,0:T(8,128)(2,1)} %param.11) | copy-start | bytes 491524
Sparse Core Ops, SparseCore 0:
  52.7 62.6 all-reduce.2
where the time goes:
time: 128 us; the launch traced here: 127 us
  waiting for transfers between devices  57.7 us (45%)
  blocking collectives  38.3 us (30%)
  between operations  14.1 us (11%)
  matrix products  10.4 us (8%)
  other arithmetic  4.13 us (3%)
  local copies, waits for them, and re-layouts  2.59 us (2%)
    psum x1, waiting for transfers between devices, shards(): total_a, total_b = lax.psum((part_a, folded_b), 'dp')  57.7 us
    psum x1, blocking collectives, shards(): lax.psum(jnp.dot(hidden, adapter_in, preferred_element_type=jnp.float32),...  21.6 us
    all_gather x1, blocking collectives, shards(): gathered = lax.all_gather(grad_out, 'tensor', axis=0, tiled=True)  16.7 us
    dot_general x3, matrix products, contract_last(): lax.dot_general(left, right, (((1,), (1,)), ((), ())), preferred_element_...  5.53 us
    mul x2, other arithmetic, shards(): return (grad_hidden, total_a * grad_scale, total_b * grad_scale)  4.13 us
    dot_general x2, matrix products, contract_first(): lax.dot_general(left, right, (((0,), (0,)), ((), ())), preferred_element_...  2.69 us
  transfers between devices with their start and end apart: 1, of which 1 were waited for; matrix products, arithmetic and copies ran while one was open for 4% of the time, Pallas kernels for 0%

commit v1 on v0

v1 whole, which is shorter than its diff:
```python
import functools

import jax
import jax.numpy as jnp
from jax import lax
from jax.experimental import pallas as pl
from jax.experimental.pallas import tpu as pltpu
from jax.sharding import PartitionSpec as P

RANK = 16
COMBOS = 16
PICKS = 2
LANES = 128
ROWS = 16
F32 = jnp.float32
BF16 = jnp.bfloat16
MESH = pl.DeviceIdType.MESH


def each(count, body):
    if count <= 8:
        for i in range(count):
            body(i)
    else:
        pl.loop(0, count)(body)


def plan(nd, nt, width, r):
    piece_rows = min(nd, r // ROWS)
    piece_cols = nd // piece_rows
    chunks = max(c for c in range(1, nt + 1) if nt % c == 0 and width % (LANES * c * piece_cols) == 0)
    return piece_rows, piece_cols, chunks


def kernel(nd, nt, hid, go, bd, ain, aout, ids, cidx, ccoef,
           gh_out, a_out, b_out,
           hid_v, ain_v, aout_v, bd_v, gath, mix, lowp, lowr, lgg, actg, paf, pab, par, pbf, pbb, pbr, acc,
           loc, loc_go, loc_ao, loc_bd, low_s, low_r, gat_s, gat_r, lg_s, lg_r, act_s, act_r,
           ra_s, ra_r, rb_s, rb_r, aa_s, aa_r, bz_s, bz_r, bx_s, bx_r, bc_s, bc_r):
    d, z = lax.axis_index("dp"), lax.axis_index("tensor")
    tg, width = go.shape
    tokens, ff = hid.shape
    r = ain.shape[1]
    piece_rows, piece_cols, chunks = plan(nd, nt, width, r)
    dc = width // chunks
    dcp = dc // piece_cols
    zc = lax.rem(z, chunks)
    zbase = z - zc
    nc = nd // 2
    chip, core = d // 2, lax.rem(d, 2)
    a_rows = pab.shape[1]

    def columns(k):
        return pl.ds(pl.multiple_of(lax.rem(zc + k, chunks) * dc, LANES), dc)

    def zpeer(i):
        return lax.rem(z + i + 1, nt)

    def zfrom(i):
        return lax.rem(z + nt - i - 1, nt)

    def dpeer(i):
        return lax.rem(d + i + 1, nd)

    def dfrom(i):
        return lax.rem(d + nd - i - 1, nd)

    def remote(src, dst, send, recv, **where):
        return pltpu.make_async_remote_copy(
            src_ref=src, dst_ref=dst, send_sem=send, recv_sem=recv, device_id=where, device_id_type=MESH)

    c_hid = pltpu.make_async_copy(hid, hid_v, loc.at[0])
    c_ain = pltpu.make_async_copy(ain, ain_v, loc.at[1])

    def c_go(q):
        return pltpu.make_async_copy(go.at[:, columns(q)], gath.at[q, z], loc_go.at[q])

    def c_ao(q):
        return pltpu.make_async_copy(aout.at[:, columns(q)], aout_v.at[q], loc_ao.at[q])

    def c_bd(q):
        return pltpu.make_async_copy(bd.at[:, columns(q)], bd_v.at[q], loc_bd.at[q])

    c_hid.start()
    c_ain.start()
    each(chunks, lambda q: c_go(q).start())
    each(chunks, lambda q: c_ao(q).start())
    each(chunks, lambda q: c_bd(q).start())

    barrier = pltpu.get_barrier_semaphore()
    each(nt - 1, lambda i: pl.semaphore_signal(barrier, inc=1, device_id={"tensor": zpeer(i)}, device_id_type=MESH))
    each(nd - 1, lambda i: pl.semaphore_signal(barrier, inc=1, device_id={"dp": dpeer(i)}, device_id_type=MESH))

    row = lax.broadcasted_iota(jnp.int32, (r, COMBOS), 0)
    table = jnp.zeros((r, COMBOS), F32)
    for p in range(PICKS):
        first = cidx[p:p + 1, :] * RANK
        table = table + jnp.where((row >= first) & (row < first + RANK), ccoef[p:p + 1, :], 0.0)
    one_hot = (lax.broadcasted_iota(jnp.int32, (COMBOS, tokens), 0) == ids[...]).astype(F32)
    mix_t = jnp.dot(table, one_hot, precision=lax.Precision.HIGHEST, preferred_element_type=F32)
    mix[...] = mix_t.T.reshape(nt, tg, r)

    c_hid.wait()
    c_ain.wait()
    lowp[...] = jnp.dot(hid_v[...], ain_v[...], preferred_element_type=F32).reshape(nt, tg, r)
    each(chunks, lambda q: c_go(q).wait())

    pl.semaphore_wait(barrier, nt + nd - 2)

    def low_copy(i):
        return remote(lowp.at[zpeer(i)], lowr.at[i], low_s.at[i], low_r.at[i], tensor=zpeer(i))

    each(nt - 1, lambda i: low_copy(i).start())

    def gather_send(q, i):
        mine = lax.rem(lax.rem(zpeer(i), chunks) + q + chunks - zc, chunks)
        return remote(gath.at[mine, z], gath.at[q, z], gat_s.at[q, i], gat_r.at[q, i], tensor=zpeer(i))

    def gather_recv(q, i):
        return remote(gath.at[q, zfrom(i)], gath.at[q, zfrom(i)], gat_s.at[q, i], gat_r.at[q, i], tensor=zpeer(i))

    each(nt - 1, lambda i: gather_send(0, i).start())

    low = jnp.zeros((tg, r), F32)
    for q in range(chunks):
        c_ao(q).wait()
        low = low + lax.dot_general(gath[q, z], aout_v[q], (((1,), (1,)), ((), ())), preferred_element_type=F32)
    lgg[z] = low * mix[z]

    def lg_send(i):
        return remote(lgg.at[z], lgg.at[z], lg_s.at[i], lg_r.at[i], tensor=zpeer(i))

    def lg_recv(i):
        return remote(lgg.at[zfrom(i)], lgg.at[zfrom(i)], lg_s.at[i], lg_r.at[i], tensor=zpeer(i))

    each(nt - 1, lambda i: lg_send(i).start())

    actg[z] = lowp[z]

    def low_add(i):
        low_copy(i).wait_recv()
        actg[z] += lowr[i]

    each(nt - 1, low_add)
    actg[z] = actg[z] * mix[z]

    def act_send(i):
        return remote(actg.at[z], actg.at[z], act_s.at[i], act_r.at[i], tensor=zpeer(i))

    def act_recv(i):
        return remote(actg.at[zfrom(i)], actg.at[zfrom(i)], act_s.at[i], act_r.at[i], tensor=zpeer(i))

    each(nt - 1, lambda i: act_send(i).start())
    for q in range(1, chunks):
        each(nt - 1, lambda i: gather_send(q, i).start())

    each(nt - 1, lambda i: lg_recv(i).wait_recv())
    low_grads = lgg[...].reshape(tokens, r).astype(BF16)
    part_a = lax.dot_general(hid_v[...], low_grads, (((0,), (0,)), ((), ())), preferred_element_type=F32)
    if nd * a_rows != ff:
        part_a = jnp.concatenate([part_a, jnp.zeros((nd * a_rows - ff, r), F32)], axis=0)
    part_a = part_a.reshape(nd, a_rows, r)
    paf[...] = part_a
    pab[...] = part_a.astype(BF16)

    def ra_copy(i):
        return remote(pab.at[dpeer(i)], par.at[i], ra_s.at[i], ra_r.at[i], dp=dpeer(i))

    each(nd - 1, lambda i: ra_copy(i).start())

    each(nt - 1, lambda i: act_recv(i).wait_recv())
    each(nt - 1, lambda i: gather_recv(0, i).wait_recv())

    def gathered(q):
        return gath[q].astype(F32).reshape(tokens, dc).astype(BF16)

    acts = actg[...].reshape(tokens, r).astype(BF16)
    grads = gathered(0)
    part_b = lax.dot_general(acts, grads, (((0,), (0,)), ((), ())), preferred_element_type=F32)
    for i in range(nd):
        top, left = (i % piece_rows) * ROWS, (i // piece_rows) * dcp
        piece = part_b[top:top + ROWS, left:left + dcp]
        pbf[i] = piece
        pbb[i] = piece.astype(BF16)

    def rb_copy(i):
        return remote(pbb.at[dpeer(i)], pbr.at[i], rb_s.at[i], rb_r.at[i], dp=dpeer(i))

    each(nd - 1, lambda i: rb_copy(i).start())

    def product(q, grads):
        c_bd(q).wait()
        return lax.dot_general(grads, bd_v[q], (((1,), (1,)), ((), ())), preferred_element_type=F32)

    acc[...] = product(0, grads) + lax.dot_general(
        low_grads, ain_v[...], (((1,), (1,)), ((), ())), preferred_element_type=F32)

    def a_piece(owner):
        return a_out.at[pl.ds(pl.multiple_of(owner * a_rows, ROWS), a_rows), :]

    def aa_send(i):
        return remote(a_piece(d), a_piece(d), aa_s.at[i], aa_r.at[i], dp=dpeer(i))

    def aa_recv(i):
        return remote(a_piece(dfrom(i)), a_piece(dfrom(i)), aa_s.at[i], aa_r.at[i], dp=dpeer(i))

    def a_add(i):
        ra_copy(i).wait_recv()
        paf[d] += par[i].astype(F32)

    each(nd - 1, a_add)
    a_piece(d)[...] = paf[d].astype(BF16)
    each(nd - 1, lambda i: aa_send(i).start())

    def b_piece(owner_chip, owner_core, chunk):
        owner = owner_chip * 2 + owner_core
        top = pl.multiple_of(lax.rem(owner, piece_rows) * ROWS, ROWS)
        left = pl.multiple_of(chunk * dc + (owner // piece_rows) * dcp, LANES)
        return b_out.at[pl.ds(top, ROWS), pl.ds(left, dcp)]

    def chip_at(j):
        return lax.rem(chip + j, nc)

    def chunk_at(k):
        return lax.rem(zc + chunks - k, chunks)

    def b_add(i):
        rb_copy(i).wait_recv()
        pbf[d] += pbr[i].astype(F32)

    each(nd - 1, b_add)
    own_b = b_piece(chip, core, zc)
    own_b[...] = pbf[d].astype(BF16)

    def bz(k, part):
        return remote(part, part, bz_s.at[k], bz_r.at[k], tensor=zbase + lax.rem(zc + k + 1, chunks))

    def bx(j, k, part):
        return remote(part, part, bx_s.at[j, k], bx_r.at[j, k], dp=chip_at(j + 1) * 2 + core)

    def bc(j, k, part):
        return remote(part, part, bc_s.at[j, k], bc_r.at[j, k], dp=chip * 2 + 1 - core)

    each(chunks - 1, lambda k: bz(k, own_b).start())
    each(nc - 1, lambda j: bx(j, 0, own_b).start())
    bc(0, 0, own_b).start()

    if chunks > 1:
        each(nt - 1, lambda i: gather_recv(1, i).wait_recv())
        acc[...] += product(1, gathered(1))

    for k in range(1, chunks):
        part = b_piece(chip, core, chunk_at(k))
        bz(k - 1, part).wait_recv()
        each(nc - 1, lambda j: bx(j, k, part).start())
        bc(0, k, part).start()

    for q in range(2, chunks):
        each(nt - 1, lambda i: gather_recv(q, i).wait_recv())
        acc[...] += product(q, gathered(q))
    gh_out[...] = acc[...].astype(BF16)

    for k in range(chunks):
        def pass_on(j):
            part = b_piece(lax.rem(chip + nc - j - 1, nc), core, chunk_at(k))
            bx(j, k, part).wait_recv()
            bc(j + 1, k, part).start()

        each(nc - 1, pass_on)

    each(nd - 1, lambda i: aa_recv(i).wait_recv())
    for k in range(chunks):
        each(nc, lambda j: bc(j, k, b_piece(lax.rem(chip + nc - j, nc), 1 - core, chunk_at(k))).wait_recv())

    def z_sends(i):
        low_copy(i).wait_send()
        lg_send(i).wait_send()
        act_send(i).wait_send()
        for q in range(chunks):
            gather_send(q, i).wait_send()

    each(nt - 1, z_sends)

    def d_sends(i):
        ra_copy(i).wait_send()
        rb_copy(i).wait_send()
        aa_send(i).wait_send()

    each(nd - 1, d_sends)
    each(chunks - 1, lambda k: bz(k, own_b).wait_send())
    for k in range(chunks):
        each(nc - 1, lambda j: bx(j, k, b_piece(chip, core, chunk_at(k))).wait_send())
        each(nc, lambda j: bc(j, k, b_piece(lax.rem(chip + nc - j, nc), core, chunk_at(k))).wait_send())


def shards(nd, nt, hidden, grad_out, base_down, adapter_in, adapter_out, mix_ids, comp_index, comp_coef):
    tokens, ff = hidden.shape
    tg, width = grad_out.shape
    r = adapter_in.shape[1]
    piece_rows, piece_cols, chunks = plan(nd, nt, width, r)
    dc = width // chunks
    dcp = dc // piece_cols
    a_rows = -(-ff // (nd * ROWS)) * ROWS
    grad_scale = float(tokens * nd) ** (-0.5)
    hbm = pl.BlockSpec(memory_space=pl.ANY)
    vmem = pl.BlockSpec(memory_space=pltpu.VMEM)
    dma = pltpu.SemaphoreType.DMA
    zs, ds = max(nt - 1, 1), max(nd - 1, 1)
    scratch = [
        pltpu.VMEM((tokens, ff), BF16), pltpu.VMEM((ff, r), BF16), pltpu.VMEM((chunks, r, dc), BF16),
        pltpu.VMEM((chunks, ff, dc), BF16), pltpu.VMEM((chunks, nt, tg, dc), BF16),
        pltpu.VMEM((nt, tg, r), F32), pltpu.VMEM((nt, tg, r), F32), pltpu.VMEM((zs, tg, r), F32),
        pltpu.VMEM((nt, tg, r), F32), pltpu.VMEM((nt, tg, r), F32),
        pltpu.VMEM((nd, a_rows, r), F32), pltpu.VMEM((nd, a_rows, r), BF16), pltpu.VMEM((ds, a_rows, r), BF16),
        pltpu.VMEM((nd, ROWS, dcp), F32), pltpu.VMEM((nd, ROWS, dcp), BF16), pltpu.VMEM((ds, ROWS, dcp), BF16),
        pltpu.VMEM((tokens, ff), F32),
        dma((2,)), dma((chunks,)), dma((chunks,)), dma((chunks,)),
        dma((zs,)), dma((zs,)), dma((chunks, zs)), dma((chunks, zs)), dma((zs,)), dma((zs,)), dma((zs,)), dma((zs,)),
        dma((ds,)), dma((ds,)), dma((ds,)), dma((ds,)), dma((ds,)), dma((ds,)),
        dma((chunks,)), dma((chunks,)), dma((nd // 2, chunks)), dma((nd // 2, chunks)),
        dma((nd // 2, chunks)), dma((nd // 2, chunks)),
    ]
    grad_hidden, sum_a, sum_b = pl.pallas_call(
        functools.partial(kernel, nd, nt),
        out_shape=(
            jax.ShapeDtypeStruct((tokens, ff), BF16),
            jax.ShapeDtypeStruct((nd * a_rows, r), BF16),
            jax.ShapeDtypeStruct((r, width), BF16),
        ),
        in_specs=[hbm] * 5 + [vmem] * 3,
        out_specs=(vmem, vmem, vmem),
        scratch_shapes=scratch,
        compiler_params=pltpu.CompilerParams(
            collective_id=0, has_side_effects=True, vmem_limit_bytes=48 * 1024 * 1024),
    )(hidden, grad_out, base_down, adapter_in, adapter_out, mix_ids.reshape(1, tokens), comp_index.T, comp_coef.T)
    return grad_hidden, sum_a[:ff].astype(F32) * grad_scale, sum_b.astype(F32) * grad_scale


def solution(mesh):
    in_specs = (
        P("dp", "tensor"),
        P(("dp", "tensor"), None),
        P("tensor", None),
        P("tensor", None),
        P(),
        P("dp"),
        P(),
        P(),
    )
    out_specs = (P("dp", "tensor"), P("tensor", None), P())
    body = functools.partial(shards, mesh.shape["dp"], mesh.shape["tensor"])
    return jax.shard_map(body, mesh=mesh, in_specs=in_specs, out_specs=out_specs, check_vma=False)
```

time: 128 us -> 46.4 us (0.36)
  waiting for transfers between devices: 57.7 us -> 0 us
  blocking collectives: 38.3 us -> 0 us
  Pallas kernels: 0 us -> 36.6 us
  between operations: 14.1 us -> 0.66 us
  matrix products: 10.4 us -> 0 us
  local copies, waits for them, and re-layouts: 2.59 us -> 6.62 us
  other arithmetic: 4.13 us -> 2.3 us
    psum x1 -> x0, waiting for transfers between devices: 57.7 us -> none  [shards(): total_a, total_b = lax.psum((part_a, folded_b), 'dp')]
    pallas_call x0 -> x1, Pallas kernels: none -> 36.6 us  [shards(): pl.pallas_call(functools.partial(kernel, nd, nt), out_shape=(jax.ShapeDty...]
    psum x1 -> x0, blocking collectives: 21.6 us -> none  [shards(): lax.psum(jnp.dot(hidden, adapter_in, preferred_element_type=jnp.float32),...]
    all_gather x1 -> x0, blocking collectives: 16.7 us -> none  [shards(): gathered = lax.all_gather(grad_out, 'tensor', axis=0, tiled=True)]
    dot_general x7 -> x0, matrix products: 10.4 us -> none  [the longest x3 5.53 us: contract_last(): lax.dot_general(left, right, (((1,), (1,)), ((), ())), preferred_element_...]
    unnamed x7 -> x15, local copies, waits for them, and re-layouts: 0.91 us -> 6.62 us
    mul x2, other arithmetic: 4.13 us -> 2.3 us  [the longest x1 1.55 us: shards(): sum_b.astype(F32) * grad_scale]
  transfers between devices with their start and end apart: 1 -> 0, of which waited for: 1 -> 0; matrix products, arithmetic and copies ran while one was open for 4% -> 0% of each run, Pallas kernels for 0% -> 0%
where the time goes in v1:
time: 46.4 us; the launch traced here: 46.1 us
  Pallas kernels  36.6 us (79%)
  local copies, waits for them, and re-layouts  6.62 us (14%)
  other arithmetic  2.3 us (5%)
  between operations  0.66 us (1%)
    pallas_call x1, Pallas kernels, shards(): pl.pallas_call(functools.partial(kernel, nd, nt), out_shape=(jax.ShapeDty...  36.6 us
    unnamed x15, local copies, waits for them, and re-layouts  6.62 us
    mul x1, other arithmetic, shards(): sum_b.astype(F32) * grad_scale  1.55 us

profile of v1, /device:TPU:0, one launch (start us, length us, event | category | flops | bytes accessed | tf_op | source)
XLA Modules:
  0.0 46.1 jit_solution(10637936088673913787)
XLA Ops:
  0.6 0.0 copy-start
  0.6 1.2 %copy-done = bf16[128,4096]{1,0:T(8,128)(2,1)S(1)} copy-done((bf16[128,4096]{1,0:T(8,128)(2,1)S(1)}, bf16[128,4096]{1,0:T(8,128)(2,1)}, u32[]{:S(2)}) %copy-start) | copy-done | bytes 1048600
  1.9 0.0 copy-start.1
  1.9 0.9 %copy-done.1 = bf16[24,4096]{1,0:T(8,128)(2,1)S(1)} copy-done((bf16[24,4096]{1,0:T(8,128)(2,1)S(1)}, bf16[24,4096]{1,0:T(8,128)(2,1)}, u32[]{:S(2)}) %copy-start.1) | copy-done | bytes 196632
  2.8 0.0 copy-start.2
  2.8 0.9 %copy-done.2 = bf16[640,128]{1,0:T(8,128)(2,1)S(1)} copy-done((bf16[640,128]{1,0:T(8,128)(2,1)S(1)}, bf16[640,128]{1,0:T(8,128)(2,1)}, u32[]{:S(2)}) %copy-start.2) | copy-done | bytes 163864
  3.7 0.0 copy-start.3
  3.7 0.9 %copy-done.3 = bf16[96,640]{1,0:T(8,128)(2,1)S(1)} copy-done((bf16[96,640]{1,0:T(8,128)(2,1)S(1)}, bf16[96,640]{1,0:T(8,128)(2,1)}, u32[]{:S(2)}) %copy-start.3) | copy-done | bytes 122904
  4.6 0.0 copy-start.4
  4.6 0.7 %copy-done.4 = s32[16,2]{0,1:T(2,128)S(1)} copy-done((s32[16,2]{0,1:T(2,128)S(1)}, s32[16,2]{0,1:T(2,128)}, u32[]{:S(2)}) %copy-start.4) | copy-done | bytes 152
  5.3 0.0 copy-start.5
  5.3 0.7 %copy-done.5 = f32[16,2]{0,1:T(2,128)S(1)} copy-done((f32[16,2]{0,1:T(2,128)S(1)}, f32[16,2]{0,1:T(2,128)}, u32[]{:S(2)}) %copy-start.5) | copy-done | bytes 152
  6.0 0.0 copy-start.6
  6.0 0.7 %copy-done.6 = s32[96]{0:T(128)S(1)} copy-done((s32[96]{0:T(128)S(1)}, s32[96]{0:T(128)}, u32[]{:S(2)}) %copy-start.6) | copy-done | bytes 408
  6.6 36.6 %shard_map.103 = (bf16[96,640]{1,0:T(8,128)(2,1)S(1)}, bf16[640,128]{1,0:T(8,128)(2,1)S(1)}, bf16[128,4096]{1,0:T(8,128)(2,1)S(1)}) custom-call(bf16[96,640]{1,0:T(8,128)(2,1)S(1)} %copy-done.3, bf16[24,4096]{1,0:T(8,128)(2,1)S(1)} %copy-done.1, bf16[640,4096]{1,0:T(8,128)(2,1)} %bd.1, bf16[640,128]{1,0:T(8,128)(2,1)S(1)} %copy-done.2, ...), custom_call_target="tpu_custom_call" | custom-call | tf_op jit(solution)/shard_map/pallas_call | solution.py:323
  43.2 1.6 %convert_multiply_fusion = f32[128,4096]{1,0:T(8,128)} fusion(bf16[128,4096]{1,0:T(8,128)(2,1)S(1)} %get-tuple-element.8), kind=kLoop, calls=%fused_computation | loop fusion | flops 1048576 | bytes 3145728 | tf_op jit(solution)/shard_map/mul | solution.py:336
  44.8 0.8 %convert_multiply_fusion.1 = f32[640,128]{1,0:T(8,128)} fusion(bf16[640,128]{1,0:T(8,128)(2,1)S(1)} %get-tuple-element.7), kind=kLoop, calls=%fused_computation.1 | loop fusion | flops 163840 | bytes 491520 | tf_op jit(solution)/shard_map/mul | solution.py:336
  45.5 0.6 %copy.12 = bf16[96,640]{1,0:T(8,128)(2,1)} copy(bf16[96,640]{1,0:T(8,128)(2,1)S(1)} %get-tuple-element.12) | data formatting | bytes 245760
Async XLA Ops:
  0.6 1.2 %copy-start = (bf16[128,4096]{1,0:T(8,128)(2,1)S(1)}, bf16[128,4096]{1,0:T(8,128)(2,1)}, u32[]{:S(2)}) copy-start(bf16[128,4096]{1,0:T(8,128)(2,1)} %aout.1) | copy-start | bytes 3145732
  1.9 0.9 %copy-start.1 = (bf16[24,4096]{1,0:T(8,128)(2,1)S(1)}, bf16[24,4096]{1,0:T(8,128)(2,1)}, u32[]{:S(2)}) copy-start(bf16[24,4096]{1,0:T(8,128)(2,1)} %go.1) | copy-start | bytes 589828
  2.8 0.9 %copy-start.2 = (bf16[640,128]{1,0:T(8,128)(2,1)S(1)}, bf16[640,128]{1,0:T(8,128)(2,1)}, u32[]{:S(2)}) copy-start(bf16[640,128]{1,0:T(8,128)(2,1)} %ain.1) | copy-start | bytes 491524
  3.7 0.9 %copy-start.3 = (bf16[96,640]{1,0:T(8,128)(2,1)S(1)}, bf16[96,640]{1,0:T(8,128)(2,1)}, u32[]{:S(2)}) copy-start(bf16[96,640]{1,0:T(8,128)(2,1)} %hid.1) | copy-start | bytes 368644
  4.6 0.7 %copy-start.4 = (s32[16,2]{0,1:T(2,128)S(1)}, s32[16,2]{0,1:T(2,128)}, u32[]{:S(2)}) copy-start(s32[16,2]{0,1:T(2,128)} %param.14) | copy-start | bytes 388
  5.3 0.7 %copy-start.5 = (f32[16,2]{0,1:T(2,128)S(1)}, f32[16,2]{0,1:T(2,128)}, u32[]{:S(2)}) copy-start(f32[16,2]{0,1:T(2,128)} %param.15) | copy-start | bytes 388
  6.0 0.7 %copy-start.6 = (s32[96]{0:T(128)S(1)}, s32[96]{0:T(128)}, u32[]{:S(2)}) copy-start(s32[96]{0:T(128)} %param.13) | copy-start | bytes 1156

commit v2 on v1

--- a/solution.py
+++ b/solution.py
@@ -34,8 +34,8 @@
 
 def kernel(nd, nt, hid, go, bd, ain, aout, ids, cidx, ccoef,
            gh_out, a_out, b_out,
-           hid_v, ain_v, aout_v, bd_v, gath, mix, lowp, lowr, lgg, actg, paf, pab, par, pbf, pbb, pbr, acc,
-           loc, loc_go, loc_ao, loc_bd, low_s, low_r, gat_s, gat_r, lg_s, lg_r, act_s, act_r,
+           hid_v, ain_v, ids_v, cidx_v, ccoef_v, aout_v, bd_v, gath, mix, lowp, lowr, lgg, actg, paf, pab, par, pbf, pbb, pbr, acc,
+           loc, loc_go, loc_ao, loc_bd, low_s, low_r, gat_s, gat_r, fwd_s, lg_s, lg_r, act_s, act_r,
            ra_s, ra_r, rb_s, rb_r, aa_s, aa_r, bz_s, bz_r, bx_s, bx_r, bc_s, bc_r):
     d, z = lax.axis_index("dp"), lax.axis_index("tensor")
     tg, width = go.shape
@@ -50,8 +50,11 @@
     chip, core = d // 2, lax.rem(d, 2)
     a_rows = pab.shape[1]
 
+    half = (nt + 1) // 2
+    turn = 1 - 2 * (z // half)
+
     def columns(k):
-        return pl.ds(pl.multiple_of(lax.rem(zc + k, chunks) * dc, LANES), dc)
+        return pl.ds(pl.multiple_of(lax.rem(zc + turn * k + chunks, chunks) * dc, LANES), dc)
 
     def zpeer(i):
         return lax.rem(z + i + 1, nt)
@@ -81,8 +84,12 @@
     def c_bd(q):
         return pltpu.make_async_copy(bd.at[:, columns(q)], bd_v.at[q], loc_bd.at[q])
 
+    small = [pltpu.make_async_copy(src, dst, loc.at[2 + n])
+             for n, (src, dst) in enumerate(((ids, ids_v), (cidx, cidx_v), (ccoef, ccoef_v)))]
     c_hid.start()
     c_ain.start()
+    for c in small:
+        c.start()
     each(chunks, lambda q: c_go(q).start())
     each(chunks, lambda q: c_ao(q).start())
     each(chunks, lambda q: c_bd(q).start())
@@ -93,10 +100,12 @@
 
     row = lax.broadcasted_iota(jnp.int32, (r, COMBOS), 0)
     table = jnp.zeros((r, COMBOS), F32)
+    for c in small:
+        c.wait()
     for p in range(PICKS):
-        first = cidx[p:p + 1, :] * RANK
-        table = table + jnp.where((row >= first) & (row < first + RANK), ccoef[p:p + 1, :], 0.0)
-    one_hot = (lax.broadcasted_iota(jnp.int32, (COMBOS, tokens), 0) == ids[...]).astype(F32)
+        first = cidx_v[p:p + 1, :] * RANK
+        table = table + jnp.where((row >= first) & (row < first + RANK), ccoef_v[p:p + 1, :], 0.0)
+    one_hot = (lax.broadcasted_iota(jnp.int32, (COMBOS, tokens), 0) == ids_v[...]).astype(F32)
     mix_t = jnp.dot(table, one_hot, precision=lax.Precision.HIGHEST, preferred_element_type=F32)
     mix[...] = mix_t.T.reshape(nt, tg, r)
 
@@ -113,19 +122,40 @@
     each(nt - 1, lambda i: low_copy(i).start())
 
     def gather_send(q, i):
-        mine = lax.rem(lax.rem(zpeer(i), chunks) + q + chunks - zc, chunks)
+        there = zpeer(i)
+        chunk = lax.rem(lax.rem(there, chunks) + (1 - 2 * (there // half)) * q + chunks, chunks)
+        mine = lax.rem(turn * (chunk - zc) + chunks, chunks)
         return remote(gath.at[mine, z], gath.at[q, z], gat_s.at[q, i], gat_r.at[q, i], tensor=zpeer(i))
 
     def gather_recv(q, i):
         return remote(gath.at[q, zfrom(i)], gath.at[q, zfrom(i)], gat_s.at[q, i], gat_r.at[q, i], tensor=zpeer(i))
 
-    each(nt - 1, lambda i: gather_send(0, i).start())
+    def if_direct(q, i, act):
+        if q == 0 or nt < 3:
+            act()
+        else:
+            pl.when(jnp.logical_not(((z == 0) & (i == nt - 2)) | ((z == nt - 1) & (i == 0))))(act)
+
+    def gather_start(q):
+        each(nt - 1, lambda i: if_direct(q, i, lambda: gather_send(q, i).start()))
+
+    def passing(q, act):
+        if nt >= 3 and q + 1 < chunks:
+            for side, (via, src, end, i) in enumerate(((nt - 2, 0, nt - 1, nt - 2), (1, nt - 1, 0, 0))):
+                pl.when(z == via)(functools.partial(act, remote(
+                    gath.at[q, src], gath.at[q + 1, src], fwd_s.at[q, side], gat_r.at[q + 1, i], tensor=end)))
+
+    def arrive(q):
+        each(nt - 1, lambda i: gather_recv(q, i).wait_recv())
+        passing(q, lambda c: c.start())
+
+    gather_start(0)
 
     low = jnp.zeros((tg, r), F32)
     for q in range(chunks):
         c_ao(q).wait()
         low = low + lax.dot_general(gath[q, z], aout_v[q], (((1,), (1,)), ((), ())), preferred_element_type=F32)
-    lgg[z] = low * mix[z]
+    lgg[z] = (low * mix[z]).astype(BF16)
 
     def lg_send(i):
         return remote(lgg.at[z], lgg.at[z], lg_s.at[i], lg_r.at[i], tensor=zpeer(i))
@@ -135,14 +165,12 @@
 
     each(nt - 1, lambda i: lg_send(i).start())
 
-    actg[z] = lowp[z]
-
     def low_add(i):
         low_copy(i).wait_recv()
-        actg[z] += lowr[i]
+        lowp[z] += lowr[i]
 
     each(nt - 1, low_add)
-    actg[z] = actg[z] * mix[z]
+    actg[z] = (lowp[z] * mix[z]).astype(BF16)
 
     def act_send(i):
         return remote(actg.at[z], actg.at[z], act_s.at[i], act_r.at[i], tensor=zpeer(i))
@@ -151,11 +179,11 @@
         return remote(actg.at[zfrom(i)], actg.at[zfrom(i)], act_s.at[i], act_r.at[i], tensor=zpeer(i))
 
     each(nt - 1, lambda i: act_send(i).start())
-    for q in range(1, chunks):
-        each(nt - 1, lambda i: gather_send(q, i).start())
+    if chunks > 1:
+        gather_start(1)
 
     each(nt - 1, lambda i: lg_recv(i).wait_recv())
-    low_grads = lgg[...].reshape(tokens, r).astype(BF16)
+    low_grads = lgg[...].astype(F32).reshape(tokens, r).astype(BF16)
     part_a = lax.dot_general(hid_v[...], low_grads, (((0,), (0,)), ((), ())), preferred_element_type=F32)
     if nd * a_rows != ff:
         part_a = jnp.concatenate([part_a, jnp.zeros((nd * a_rows - ff, r), F32)], axis=0)
@@ -169,12 +197,12 @@
     each(nd - 1, lambda i: ra_copy(i).start())
 
     each(nt - 1, lambda i: act_recv(i).wait_recv())
-    each(nt - 1, lambda i: gather_recv(0, i).wait_recv())
+    arrive(0)
 
     def gathered(q):
         return gath[q].astype(F32).reshape(tokens, dc).astype(BF16)
 
-    acts = actg[...].reshape(tokens, r).astype(BF16)
+    acts = actg[...].astype(F32).reshape(tokens, r).astype(BF16)
     grads = gathered(0)
     part_b = lax.dot_general(acts, grads, (((0,), (0,)), ((), ())), preferred_element_type=F32)
     for i in range(nd):
@@ -245,28 +273,35 @@
     each(nc - 1, lambda j: bx(j, 0, own_b).start())
     bc(0, 0, own_b).start()
 
+    for q in range(2, chunks):
+        gather_start(q)
+
+    def pass_on(k):
+        def one(j):
+            part = b_piece(lax.rem(chip + nc - j - 1, nc), core, chunk_at(k))
+            bx(j, k, part).wait_recv()
+            bc(j + 1, k, part).start()
+
+        each(nc - 1, one)
+
     if chunks > 1:
-        each(nt - 1, lambda i: gather_recv(1, i).wait_recv())
+        arrive(1)
         acc[...] += product(1, gathered(1))
-
+    pass_on(0)
     for k in range(1, chunks):
         part = b_piece(chip, core, chunk_at(k))
         bz(k - 1, part).wait_recv()
         each(nc - 1, lambda j: bx(j, k, part).start())
         bc(0, k, part).start()
-
-    for q in range(2, chunks):
-        each(nt - 1, lambda i: gather_recv(q, i).wait_recv())
+    if chunks > 2:
+        arrive(2)
+        acc[...] += product(2, gathered(2))
+    for k in range(1, chunks):
+        pass_on(k)
+    for q in range(3, chunks):
+        arrive(q)
         acc[...] += product(q, gathered(q))
     gh_out[...] = acc[...].astype(BF16)
-
-    for k in range(chunks):
-        def pass_on(j):
-            part = b_piece(lax.rem(chip + nc - j - 1, nc), core, chunk_at(k))
-            bx(j, k, part).wait_recv()
-            bc(j + 1, k, part).start()
-
-        each(nc - 1, pass_on)
 
     each(nd - 1, lambda i: aa_recv(i).wait_recv())
     for k in range(chunks):
@@ -277,9 +312,11 @@
         lg_send(i).wait_send()
         act_send(i).wait_send()
         for q in range(chunks):
-            gather_send(q, i).wait_send()
+            if_direct(q, i, functools.partial(lambda q: gather_send(q, i).wait_send(), q))
 
     each(nt - 1, z_sends)
+    for q in range(chunks):
+        passing(q, lambda c: c.wait_send())
 
     def d_sends(i):
         ra_copy(i).wait_send()
@@ -291,6 +328,22 @@
     for k in range(chunks):
         each(nc - 1, lambda j: bx(j, k, b_piece(chip, core, chunk_at(k))).wait_send())
         each(nc, lambda j: bc(j, k, b_piece(lax.rem(chip + nc - j, nc), core, chunk_at(k))).wait_send())
+
+
+def finish(scale, gh, a, b, gh_out, a_out, b_out, a_v, b_v, sem):
+    copies = [pltpu.make_async_copy(gh, gh_out, sem.at[0])]
+    copies[0].start()
+    step = b.shape[0] // 4
+    for n in range(4):
+        rows = pl.ds(n * step, step)
+        b_v[rows, :] = b[rows, :].astype(F32) * scale
+        copies.append(pltpu.make_async_copy(b_v.at[rows, :], b_out.at[rows, :], sem.at[1 + n]))
+        copies[-1].start()
+    a_v[...] = a[:a_v.shape[0], :].astype(F32) * scale
+    copies.append(pltpu.make_async_copy(a_v, a_out, sem.at[5]))
+    copies[-1].start()
+    for c in copies:
+        c.wait()
 
 
 def shards(nd, nt, hidden, grad_out, base_down, adapter_in, adapter_out, mix_ids, comp_index, comp_coef):
@@ -302,20 +355,22 @@
     dcp = dc // piece_cols
     a_rows = -(-ff // (nd * ROWS)) * ROWS
     grad_scale = float(tokens * nd) ** (-0.5)
-    hbm = pl.BlockSpec(memory_space=pl.ANY)
+    hbm = pl.BlockSpec(memory_space=pltpu.HBM)
     vmem = pl.BlockSpec(memory_space=pltpu.VMEM)
     dma = pltpu.SemaphoreType.DMA
     zs, ds = max(nt - 1, 1), max(nd - 1, 1)
     scratch = [
-        pltpu.VMEM((tokens, ff), BF16), pltpu.VMEM((ff, r), BF16), pltpu.VMEM((chunks, r, dc), BF16),
+        pltpu.VMEM((tokens, ff), BF16), pltpu.VMEM((ff, r), BF16),
+        pltpu.VMEM((1, tokens), jnp.int32), pltpu.VMEM((PICKS, COMBOS), jnp.int32), pltpu.VMEM((PICKS, COMBOS), F32),
+        pltpu.VMEM((chunks, r, dc), BF16),
         pltpu.VMEM((chunks, ff, dc), BF16), pltpu.VMEM((chunks, nt, tg, dc), BF16),
         pltpu.VMEM((nt, tg, r), F32), pltpu.VMEM((nt, tg, r), F32), pltpu.VMEM((zs, tg, r), F32),
-        pltpu.VMEM((nt, tg, r), F32), pltpu.VMEM((nt, tg, r), F32),
+        pltpu.VMEM((nt, tg, r), BF16), pltpu.VMEM((nt, tg, r), BF16),
         pltpu.VMEM((nd, a_rows, r), F32), pltpu.VMEM((nd, a_rows, r), BF16), pltpu.VMEM((ds, a_rows, r), BF16),
         pltpu.VMEM((nd, ROWS, dcp), F32), pltpu.VMEM((nd, ROWS, dcp), BF16), pltpu.VMEM((ds, ROWS, dcp), BF16),
         pltpu.VMEM((tokens, ff), F32),
-        dma((2,)), dma((chunks,)), dma((chunks,)), dma((chunks,)),
-        dma((zs,)), dma((zs,)), dma((chunks, zs)), dma((chunks, zs)), dma((zs,)), dma((zs,)), dma((zs,)), dma((zs,)),
+        dma((5,)), dma((chunks,)), dma((chunks,)), dma((chunks,)),
+        dma((zs,)), dma((zs,)), dma((chunks, zs)), dma((chunks, zs)), dma((chunks, 2)), dma((zs,)), dma((zs,)), dma((zs,)), dma((zs,)),
         dma((ds,)), dma((ds,)), dma((ds,)), dma((ds,)), dma((ds,)), dma((ds,)),
         dma((chunks,)), dma((chunks,)), dma((nd // 2, chunks)), dma((nd // 2, chunks)),
         dma((nd // 2, chunks)), dma((nd // 2, chunks)),
@@ -327,13 +382,24 @@
             jax.ShapeDtypeStruct((nd * a_rows, r), BF16),
             jax.ShapeDtypeStruct((r, width), BF16),
         ),
-        in_specs=[hbm] * 5 + [vmem] * 3,
+        in_specs=[hbm] * 8,
         out_specs=(vmem, vmem, vmem),
         scratch_shapes=scratch,
         compiler_params=pltpu.CompilerParams(
             collective_id=0, has_side_effects=True, vmem_limit_bytes=48 * 1024 * 1024),
     )(hidden, grad_out, base_down, adapter_in, adapter_out, mix_ids.reshape(1, tokens), comp_index.T, comp_coef.T)
-    return grad_hidden, sum_a[:ff].astype(F32) * grad_scale, sum_b.astype(F32) * grad_scale
+    return pl.pallas_call(
+        functools.partial(finish, grad_scale),
+        out_shape=(
+            jax.ShapeDtypeStruct((tokens, ff), BF16),
+            jax.ShapeDtypeStruct((ff, r), F32),
+            jax.ShapeDtypeStruct((r, width), F32),
+        ),
+        in_specs=[vmem] * 3,
+        out_specs=(hbm, hbm, hbm),
+        scratch_shapes=[pltpu.VMEM((ff, r), F32), pltpu.VMEM((r, width), F32), dma((6,))],
+        compiler_params=pltpu.CompilerParams(vmem_limit_bytes=16 * 1024 * 1024),
+    )(grad_hidden, sum_a, sum_b)
 
 
 def solution(mesh):

time: 46.4 us -> 43.7 us (0.942)
  other arithmetic: 2.3 us -> 0 us
  local copies, waits for them, and re-layouts: 6.62 us -> 5.97 us
    mul x2 -> x0, other arithmetic: 2.3 us -> none  [the longest x1 1.55 us: shards(): sum_b.astype(F32) * grad_scale]
    pallas_call x0 -> x1, Pallas kernels: none -> 1.51 us  [shards(): pl.pallas_call(functools.partial(finish, grad_scale), out_shape=(jax.Shap...]
    pallas_call x1, Pallas kernels: 36.6 us -> 35.3 us  [shards(): pl.pallas_call(functools.partial(kernel, nd, nt), out_shape=(jax.ShapeDty...]
    unnamed x15 -> x14, local copies, waits for them, and re-layouts: 6.62 us -> 5.97 us
where the time goes in v2:
time: 43.7 us; the launch traced here: 43.4 us
  Pallas kernels  36.8 us (84%)
  local copies, waits for them, and re-layouts  5.97 us (14%)
  between operations  0.66 us (2%)
    pallas_call x1, Pallas kernels, shards(): pl.pallas_call(functools.partial(kernel, nd, nt), out_shape=(jax.ShapeDty...  35.3 us
    unnamed x14, local copies, waits for them, and re-layouts  5.97 us
    pallas_call x1, Pallas kernels, shards(): pl.pallas_call(functools.partial(finish, grad_scale), out_shape=(jax.Shap...  1.51 us

profile of v2, /device:TPU:0, one launch (start us, length us, event | category | flops | bytes accessed | tf_op | source)
XLA Modules:
  0.0 43.4 jit_solution(6625081103136558866)
XLA Ops:
  0.6 0.0 copy-start
  0.6 1.2 %copy-done = bf16[128,4096]{1,0:T(8,128)(2,1)S(1)} copy-done((bf16[128,4096]{1,0:T(8,128)(2,1)S(1)}, bf16[128,4096]{1,0:T(8,128)(2,1)}, u32[]{:S(2)}) %copy-start) | copy-done | bytes 1048600
  1.9 0.0 copy-start.1
  1.9 0.9 %copy-done.1 = bf16[24,4096]{1,0:T(8,128)(2,1)S(1)} copy-done((bf16[24,4096]{1,0:T(8,128)(2,1)S(1)}, bf16[24,4096]{1,0:T(8,128)(2,1)}, u32[]{:S(2)}) %copy-start.1) | copy-done | bytes 196632
  2.8 0.0 copy-start.2
  2.8 0.9 %copy-done.2 = bf16[640,128]{1,0:T(8,128)(2,1)S(1)} copy-done((bf16[640,128]{1,0:T(8,128)(2,1)S(1)}, bf16[640,128]{1,0:T(8,128)(2,1)}, u32[]{:S(2)}) %copy-start.2) | copy-done | bytes 163864
  3.7 0.0 copy-start.3
  3.7 0.9 %copy-done.3 = bf16[96,640]{1,0:T(8,128)(2,1)S(1)} copy-done((bf16[96,640]{1,0:T(8,128)(2,1)S(1)}, bf16[96,640]{1,0:T(8,128)(2,1)}, u32[]{:S(2)}) %copy-start.3) | copy-done | bytes 122904
  4.6 0.0 copy-start.4
  4.6 0.7 %copy-done.4 = s32[16,2]{0,1:T(2,128)S(1)} copy-done((s32[16,2]{0,1:T(2,128)S(1)}, s32[16,2]{0,1:T(2,128)}, u32[]{:S(2)}) %copy-start.4) | copy-done | bytes 152
  5.3 0.0 copy-start.5
  5.3 0.7 %copy-done.5 = f32[16,2]{0,1:T(2,128)S(1)} copy-done((f32[16,2]{0,1:T(2,128)S(1)}, f32[16,2]{0,1:T(2,128)}, u32[]{:S(2)}) %copy-start.5) | copy-done | bytes 152
  6.0 0.0 copy-start.6
  6.0 0.7 %copy-done.6 = s32[96]{0:T(128)S(1)} copy-done((s32[96]{0:T(128)S(1)}, s32[96]{0:T(128)}, u32[]{:S(2)}) %copy-start.6) | copy-done | bytes 408
  6.6 35.3 %shard_map.103 = (bf16[96,640]{1,0:T(8,128)(2,1)S(1)}, bf16[640,128]{1,0:T(8,128)(2,1)S(1)}, bf16[128,4096]{1,0:T(8,128)(2,1)S(1)}) custom-call(bf16[96,640]{1,0:T(8,128)(2,1)S(1)} %copy-done.3, bf16[24,4096]{1,0:T(8,128)(2,1)S(1)} %copy-done.1, bf16[640,4096]{1,0:T(8,128)(2,1)} %bd.1, bf16[640,128]{1,0:T(8,128)(2,1)S(1)} %copy-done.2, ...), custom_call_target="tpu_custom_call" | custom-call | tf_op jit(solution)/shard_map/pallas_call | solution.py:378
  41.9 1.5 %shard_map.104 = (bf16[96,640]{1,0:T(8,128)(2,1)}, f32[640,128]{1,0:T(8,128)}, f32[128,4096]{1,0:T(8,128)}) custom-call(bf16[96,640]{1,0:T(8,128)(2,1)S(1)} %get-tuple-element.6.gh, bf16[640,128]{1,0:T(8,128)(2,1)S(1)} %get-tuple-element.7.a, bf16[128,4096]{1,0:T(8,128)(2,1)S(1)} %get-tuple-element.8.b), custom_call_target="tpu_custom_call" | custom-call | tf_op jit(solution)/shard_map/pallas_call | solution.py:391
Async XLA Ops:
  0.6 1.2 %copy-start = (bf16[128,4096]{1,0:T(8,128)(2,1)S(1)}, bf16[128,4096]{1,0:T(8,128)(2,1)}, u32[]{:S(2)}) copy-start(bf16[128,4096]{1,0:T(8,128)(2,1)} %aout.1) | copy-start | bytes 3145732
  1.9 0.9 %copy-start.1 = (bf16[24,4096]{1,0:T(8,128)(2,1)S(1)}, bf16[24,4096]{1,0:T(8,128)(2,1)}, u32[]{:S(2)}) copy-start(bf16[24,4096]{1,0:T(8,128)(2,1)} %go.1) | copy-start | bytes 589828
  2.8 0.9 %copy-start.2 = (bf16[640,128]{1,0:T(8,128)(2,1)S(1)}, bf16[640,128]{1,0:T(8,128)(2,1)}, u32[]{:S(2)}) copy-start(bf16[640,128]{1,0:T(8,128)(2,1)} %ain.1) | copy-start | bytes 491524
  3.7 0.9 %copy-start.3 = (bf16[96,640]{1,0:T(8,128)(2,1)S(1)}, bf16[96,640]{1,0:T(8,128)(2,1)}, u32[]{:S(2)}) copy-start(bf16[96,640]{1,0:T(8,128)(2,1)} %hid.1) | copy-start | bytes 368644
  4.6 0.7 %copy-start.4 = (s32[16,2]{0,1:T(2,128)S(1)}, s32[16,2]{0,1:T(2,128)}, u32[]{:S(2)}) copy-start(s32[16,2]{0,1:T(2,128)} %param.14) | copy-start | bytes 388
  5.3 0.7 %copy-start.5 = (f32[16,2]{0,1:T(2,128)S(1)}, f32[16,2]{0,1:T(2,128)}, u32[]{:S(2)}) copy-start(f32[16,2]{0,1:T(2,128)} %param.15) | copy-start | bytes 388
  6.0 0.7 %copy-start.6 = (s32[96]{0:T(128)S(1)}, s32[96]{0:T(128)}, u32[]{:S(2)}) copy-start(s32[96]{0:T(128)} %param.13) | copy-start | bytes 1156

commit v3 on v2

--- a/solution.py
+++ b/solution.py
@@ -182,6 +182,26 @@
     if chunks > 1:
         gather_start(1)
 
+    each(nt - 1, lambda i: act_recv(i).wait_recv())
+    arrive(0)
+
+    def gathered(q):
+        return gath[q].astype(F32).reshape(tokens, dc).astype(BF16)
+
+    acts = actg[...].astype(F32).reshape(tokens, r).astype(BF16)
+    grads = gathered(0)
+    part_b = lax.dot_general(acts, grads, (((0,), (0,)), ((), ())), preferred_element_type=F32)
+    for i in range(nd):
+        top, left = (i % piece_rows) * ROWS, (i // piece_rows) * dcp
+        piece = part_b[top:top + ROWS, left:left + dcp]
+        pbf[i] = piece
+        pbb[i] = piece.astype(BF16)
+
+    def rb_copy(i):
+        return remote(pbb.at[dpeer(i)], pbr.at[i], rb_s.at[i], rb_r.at[i], dp=dpeer(i))
+
+    each(nd - 1, lambda i: rb_copy(i).start())
+
     each(nt - 1, lambda i: lg_recv(i).wait_recv())
     low_grads = lgg[...].astype(F32).reshape(tokens, r).astype(BF16)
     part_a = lax.dot_general(hid_v[...], low_grads, (((0,), (0,)), ((), ())), preferred_element_type=F32)
@@ -196,26 +216,6 @@
 
     each(nd - 1, lambda i: ra_copy(i).start())
 
-    each(nt - 1, lambda i: act_recv(i).wait_recv())
-    arrive(0)
-
-    def gathered(q):
-        return gath[q].astype(F32).reshape(tokens, dc).astype(BF16)
-
-    acts = actg[...].astype(F32).reshape(tokens, r).astype(BF16)
-    grads = gathered(0)
-    part_b = lax.dot_general(acts, grads, (((0,), (0,)), ((), ())), preferred_element_type=F32)
-    for i in range(nd):
-        top, left = (i % piece_rows) * ROWS, (i // piece_rows) * dcp
-        piece = part_b[top:top + ROWS, left:left + dcp]
-        pbf[i] = piece
-        pbb[i] = piece.astype(BF16)
-
-    def rb_copy(i):
-        return remote(pbb.at[dpeer(i)], pbr.at[i], rb_s.at[i], rb_r.at[i], dp=dpeer(i))
-
-    each(nd - 1, lambda i: rb_copy(i).start())
-
     def product(q, grads):
         c_bd(q).wait()
         return lax.dot_general(grads, bd_v[q], (((1,), (1,)), ((), ())), preferred_element_type=F32)
@@ -231,14 +231,6 @@
 
     def aa_recv(i):
         return remote(a_piece(dfrom(i)), a_piece(dfrom(i)), aa_s.at[i], aa_r.at[i], dp=dpeer(i))
-
-    def a_add(i):
-        ra_copy(i).wait_recv()
-        paf[d] += par[i].astype(F32)
-
-    each(nd - 1, a_add)
-    a_piece(d)[...] = paf[d].astype(BF16)
-    each(nd - 1, lambda i: aa_send(i).start())
 
     def b_piece(owner_chip, owner_core, chunk):
         owner = owner_chip * 2 + owner_core
@@ -275,6 +267,14 @@
 
     for q in range(2, chunks):
         gather_start(q)
+
+    def a_add(i):
+        ra_copy(i).wait_recv()
+        paf[d] += par[i].astype(F32)
+
+    each(nd - 1, a_add)
+    a_piece(d)[...] = paf[d].astype(BF16)
+    each(nd - 1, lambda i: aa_send(i).start())
 
     def pass_on(k):
         def one(j):
@@ -378,15 +378,15 @@
     grad_hidden, sum_a, sum_b = pl.pallas_call(
         functools.partial(kernel, nd, nt),
         out_shape=(
-            jax.ShapeDtypeStruct((tokens, ff), BF16),
-            jax.ShapeDtypeStruct((nd * a_rows, r), BF16),
-            jax.ShapeDtypeStruct((r, width), BF16),
+            pltpu.VMEM((tokens, ff), BF16),
+            pltpu.VMEM((nd * a_rows, r), BF16),
+            pltpu.VMEM((r, width), BF16),
         ),
         in_specs=[hbm] * 8,
         out_specs=(vmem, vmem, vmem),
         scratch_shapes=scratch,
         compiler_params=pltpu.CompilerParams(
-            collective_id=0, has_side_effects=True, vmem_limit_bytes=48 * 1024 * 1024),
+            collective_id=0, has_side_effects=True, vmem_limit_bytes=56 * 1024 * 1024),
     )(hidden, grad_out, base_down, adapter_in, adapter_out, mix_ids.reshape(1, tokens), comp_index.T, comp_coef.T)
     return pl.pallas_call(
         functools.partial(finish, grad_scale),

time: 43.7 us -> 36.6 us (0.84)
  local copies, waits for them, and re-layouts: 5.97 us -> 0 us
  Pallas kernels: 36.8 us -> 35.8 us
    unnamed x14 -> x0, local copies, waits for them, and re-layouts: 5.97 us -> none
    pallas_call x1, Pallas kernels: 35.3 us -> 34.3 us  [shards(): pl.pallas_call(functools.partial(kernel, nd, nt), out_shape=(pltpu.VMEM((...]
where the time goes in v3:
time: 36.6 us; the launch traced here: 36.5 us
  Pallas kernels  35.8 us (98%)
  between operations  0.64 us (2%)
    pallas_call x1, Pallas kernels, shards(): pl.pallas_call(functools.partial(kernel, nd, nt), out_shape=(pltpu.VMEM((...  34.3 us
    pallas_call x1, Pallas kernels, shards(): pl.pallas_call(functools.partial(finish, grad_scale), out_shape=(jax.Shap...  1.51 us

profile of v3, /device:TPU:0, one launch (start us, length us, event | category | flops | bytes accessed | tf_op | source)
XLA Modules:
  0.0 36.5 jit_solution(1290883883899151515)
XLA Ops:
  0.6 34.3 %shard_map.103 = (bf16[96,640]{1,0:T(8,128)(2,1)S(1)}, bf16[640,128]{1,0:T(8,128)(2,1)S(1)}, bf16[128,4096]{1,0:T(8,128)(2,1)S(1)}) custom-call(bf16[96,640]{1,0:T(8,128)(2,1)} %hid.1, bf16[24,4096]{1,0:T(8,128)(2,1)} %go.1, bf16[640,4096]{1,0:T(8,128)(2,1)} %bd.1, bf16[640,128]{1,0:T(8,128)(2,1)} %ain.1, bf16[128,4096]{1,0:T(8,128)(2,1)} %aout.1, ...), custom_call_target="tpu_custom_call" | custom-call | tf_op jit(solution)/shard_map/pallas_call | solution.py:378
  35.0 1.5 %shard_map.104 = (bf16[96,640]{1,0:T(8,128)(2,1)}, f32[640,128]{1,0:T(8,128)}, f32[128,4096]{1,0:T(8,128)}) custom-call(bf16[96,640]{1,0:T(8,128)(2,1)S(1)} %get-tuple-element.6.gh, bf16[640,128]{1,0:T(8,128)(2,1)S(1)} %get-tuple-element.7.a, bf16[128,4096]{1,0:T(8,128)(2,1)S(1)} %get-tuple-element.8.b), custom_call_target="tpu_custom_call" | custom-call | tf_op jit(solution)/shard_map/pallas_call | solution.py:391

commit v4 on v3

--- a/solution.py
+++ b/solution.py
@@ -181,6 +181,17 @@
     each(nt - 1, lambda i: act_send(i).start())
     if chunks > 1:
         gather_start(1)
+    for q in range(2, chunks):
+        gather_start(q)
+
+    each(nt - 1, lambda i: lg_recv(i).wait_recv())
+    low_grads = lgg[...].astype(F32).reshape(tokens, r).astype(BF16)
+    part_a = lax.dot_general(hid_v[...], low_grads, (((0,), (0,)), ((), ())), preferred_element_type=F32)
+    if nd * a_rows != ff:
+        part_a = jnp.concatenate([part_a, jnp.zeros((nd * a_rows - ff, r), F32)], axis=0)
+    part_a = part_a.reshape(nd, a_rows, r)
+    paf[...] = part_a
+    pab[...] = part_a.astype(BF16)
 
     each(nt - 1, lambda i: act_recv(i).wait_recv())
     arrive(0)
@@ -202,15 +213,6 @@
 
     each(nd - 1, lambda i: rb_copy(i).start())
 
-    each(nt - 1, lambda i: lg_recv(i).wait_recv())
-    low_grads = lgg[...].astype(F32).reshape(tokens, r).astype(BF16)
-    part_a = lax.dot_general(hid_v[...], low_grads, (((0,), (0,)), ((), ())), preferred_element_type=F32)
-    if nd * a_rows != ff:
-        part_a = jnp.concatenate([part_a, jnp.zeros((nd * a_rows - ff, r), F32)], axis=0)
-    part_a = part_a.reshape(nd, a_rows, r)
-    paf[...] = part_a
-    pab[...] = part_a.astype(BF16)
-
     def ra_copy(i):
         return remote(pab.at[dpeer(i)], par.at[i], ra_s.at[i], ra_r.at[i], dp=dpeer(i))
 
@@ -265,8 +267,6 @@
     each(nc - 1, lambda j: bx(j, 0, own_b).start())
     bc(0, 0, own_b).start()
 
-    for q in range(2, chunks):
-        gather_start(q)
 
     def a_add(i):
         ra_copy(i).wait_recv()

time: 36.6 us -> 36 us (0.984)
  Pallas kernels: 35.8 us -> 35.2 us
    pallas_call x1, Pallas kernels: 34.3 us -> 33.7 us  [shards(): pl.pallas_call(functools.partial(kernel, nd, nt), out_shape=(pltpu.VMEM((...]
where the time goes in v4:
time: 36 us; the launch traced here: 35.9 us
  Pallas kernels  35.2 us (98%)
  between operations  0.64 us (2%)
    pallas_call x1, Pallas kernels, shards(): pl.pallas_call(functools.partial(kernel, nd, nt), out_shape=(pltpu.VMEM((...  33.7 us
    pallas_call x1, Pallas kernels, shards(): pl.pallas_call(functools.partial(finish, grad_scale), out_shape=(jax.Shap...  1.51 us

profile of v4, /device:TPU:0, one launch (start us, length us, event | category | flops | bytes accessed | tf_op | source)
XLA Modules:
  0.0 35.9 jit_solution(15101006830870566849)
XLA Ops:
  0.6 33.7 %shard_map.103 = (bf16[96,640]{1,0:T(8,128)(2,1)S(1)}, bf16[640,128]{1,0:T(8,128)(2,1)S(1)}, bf16[128,4096]{1,0:T(8,128)(2,1)S(1)}) custom-call(bf16[96,640]{1,0:T(8,128)(2,1)} %hid.1, bf16[24,4096]{1,0:T(8,128)(2,1)} %go.1, bf16[640,4096]{1,0:T(8,128)(2,1)} %bd.1, bf16[640,128]{1,0:T(8,128)(2,1)} %ain.1, bf16[128,4096]{1,0:T(8,128)(2,1)} %aout.1, ...), custom_call_target="tpu_custom_call" | custom-call | tf_op jit(solution)/shard_map/pallas_call | solution.py:378
  34.4 1.5 %shard_map.104 = (bf16[96,640]{1,0:T(8,128)(2,1)}, f32[640,128]{1,0:T(8,128)}, f32[128,4096]{1,0:T(8,128)}) custom-call(bf16[96,640]{1,0:T(8,128)(2,1)S(1)} %get-tuple-element.6.gh, bf16[640,128]{1,0:T(8,128)(2,1)S(1)} %get-tuple-element.7.a, bf16[128,4096]{1,0:T(8,128)(2,1)S(1)} %get-tuple-element.8.b), custom_call_target="tpu_custom_call" | custom-call | tf_op jit(solution)/shard_map/pallas_call | solution.py:391
